TPU v7x, 256 devices: a whole 4x4x8 slice. The times are simulated.
256 devices in a mesh: group: 8 (over z_lo, core), section: 8 (over z_hi, x), tensor: 4 (over y).
Axes of the slice: x: 4, y: 4, z: 8 (z_hi: 2, z_lo: 4; z = z_hi * 4 + z_lo), core: 2. Of those that a mesh axis runs over, the one named last changes fastest.
Arguments:
- hidden_in: bfloat16 [256, 4096], P('group'), may hold values from -6 to 6
- queries: bfloat16 [8, 256, 4096], P('section', 'group', 'tensor'), may hold values from -5 to 5
- cache: bfloat16 [8, 256, 64, 1024], P('section', 'group', None, 'tensor'), may hold values from -5 to 5
- lengths: int32 [256], P('group'), may hold values from 2 to 63, as said below
- moves: int32 [48, 3], P('group'), may hold values from 0 to 31, as said below
- norm_gain: float32 [8, 4096], P('section'), may hold values from 0.5 to 1.5
- kv_weight: bfloat16 [8, 4096, 1024], P('section', None, 'tensor'), may hold values from -0.09375 to 0.09375
- out_weight: bfloat16 [8, 4096, 4096], P('section', 'tensor'), may hold values from -0.1875 to 0.1875
Outputs:
- layer_out: bfloat16 [8, 256, 4096], P('section', 'group', 'tensor')
- new_cache: bfloat16 [8, 256, 64, 1024], P('section', 'group', None, 'tensor')
Inputs may be any that keep to these rules, and one draw needn't show every extreme that they name: `moves`: each group's 6 rows name distinct slots of that group. They come in 3 runs of 2 rows, each run with one destination group; the runs' destinations differ from one another and from the sender, and the first run of every group goes to the group half the number of groups further on, counted round. Every group receives 6 requests, into exactly the slots whose requests left it. `lengths`: cache rows at positions from the length on are unused.
All inputs are finite; a program needn't handle non-finite values.
Results may differ from a plain program's by a relative error of at most 0.024.
Values may be sent and summed in bfloat16 or wider, within the bound.
A program may use at most 64 MiB of HBM per device.

v0:
```python
import jax
import jax.numpy as jnp
from jax import lax
from jax.sharding import PartitionSpec as P

HD = 128
PAIR = 2


def passed_along(block, axis, distance):
    devices = range(lax.axis_size(axis))
    route = [(i - distance, i) for i in devices if i - distance in devices]
    return lax.ppermute(block, axis, route)


def decode_layer(hidden, gain, kv_weight, query, cache, lengths, out_weight):
    rows = hidden.shape[0]
    ctx = cache.shape[1]
    kv_heads = cache.shape[-1] // (2 * HD)
    q_heads = query.shape[-1] // HD
    group_size = q_heads // kv_heads
    widef = hidden.astype(jnp.float32)
    normed = (widef * lax.rsqrt(jnp.mean(widef * widef, -1, keepdims=True) + 1e-06) * gain).astype(
        jnp.bfloat16
    )
    fresh = jnp.dot(normed, kv_weight, preferred_element_type=jnp.float32).astype(jnp.bfloat16)
    fresh_split = fresh.reshape(rows, kv_heads, 2, HD)
    cache_split = cache.reshape(rows, ctx, kv_heads, 2, HD)
    query_split = query.reshape(rows, kv_heads, group_size, HD)
    scale = HD ** (-0.5)
    scores = (
        jnp.einsum(
            "rhgd,rlhd->rhgl",
            query_split,
            cache_split[:, :, :, 0],
            preferred_element_type=jnp.float32,
        )
        * scale
    )
    own = (
        jnp.einsum(
            "rhgd,rhd->rhg", query_split, fresh_split[:, :, 0], preferred_element_type=jnp.float32
        )
        * scale
    )
    valid = (jnp.arange(ctx, dtype=jnp.int32)[None, :] < lengths[:, None])[:, None, None, :]
    scores = jnp.where(valid, scores, -jnp.inf)
    top = jnp.maximum(jnp.max(scores, -1), own)
    weights = jnp.where(valid, jnp.exp(scores - top[..., None]), 0.0)
    own_weight = jnp.exp(own - top)
    total = jnp.sum(weights, -1) + own_weight
    probs = (weights / total[..., None]).astype(jnp.bfloat16)
    own_prob = (own_weight / total).astype(jnp.bfloat16)
    context = jnp.einsum(
        "rhgl,rlhd->rhgd", probs, cache_split[:, :, :, 1], preferred_element_type=jnp.float32
    )
    context = context + own_prob[..., None].astype(jnp.float32) * fresh_split[:, :, 1][
        :, :, None, :
    ].astype(jnp.float32)
    context = context.astype(jnp.bfloat16).reshape(rows, q_heads * HD)
    partial_value = jnp.dot(context, out_weight, preferred_element_type=jnp.float32)
    return (widef, partial_value, fresh)


def write_fresh(cache, lengths, fresh):
    ctx = cache.shape[1]
    marked = jnp.arange(ctx, dtype=jnp.int32)[None, :] == lengths[:, None]
    return jnp.where(marked[:, :, None], fresh[:, None, :], cache)


def run_layers(
    source, query, store, lengths, gain, kv_weight, out_weight, micro, columns, column_start
):
    slots = source.shape[0]
    width = source.shape[1]
    rows = slots // micro
    section = lax.axis_index("section")
    turns = lax.axis_size("section") + micro - 1

    def advance(turn, carry):
        incoming, layer_rows, fresh_rows = carry
        batch = turn - section
        active = (batch >= 0) & (batch < micro)
        arrived_rows = incoming
        current = jnp.where(section == 0, source, arrived_rows)
        widef, partial_value, fresh = decode_layer(
            current, gain, kv_weight, query, store, lengths, out_weight
        )
        summed = lax.psum(partial_value.astype(jnp.bfloat16), "tensor").astype(jnp.float32)
        result = (widef + summed).astype(jnp.bfloat16)
        kept = lax.dynamic_slice_in_dim(result, column_start, columns, 1)
        incoming = passed_along(result, "section", 1)
        earlier = layer_rows
        layer_rows = jnp.where(active, kept, earlier)
        fresh_old = fresh_rows
        fresh_rows = jnp.where(active, fresh, fresh_old)
        return (incoming, layer_rows, fresh_rows)

    start = (
        jnp.zeros((rows, width), jnp.bfloat16),
        jnp.zeros((slots, columns), jnp.bfloat16),
        jnp.zeros((slots, store.shape[-1]), jnp.bfloat16),
    )
    ending = lax.fori_loop(0, turns, advance, start)
    return (ending[1], ending[2])


def per_device(hidden_in, queries, cache, lengths, moves, norm_gain, kv_weight, out_weight):
    slots = hidden_in.shape[0]
    groups = lax.axis_size("group")
    columns = hidden_in.shape[1] // lax.axis_size("tensor")
    column_start = lax.axis_index("tensor") * columns
    gain = norm_gain[0]
    kv_local = kv_weight[0]
    out_local = out_weight[0]
    query = queries[0]
    store = cache[0]
    sources = moves[:, 0]
    places = moves[:, 2]
    run_targets = moves[:, 1].reshape(-1, PAIR)[:, 0]
    micro = 1

    def pack(item, filler):
        shaped = item.reshape((run_targets.shape[0], PAIR) + item.shape[1:])
        blank = jnp.full((groups, PAIR) + item.shape[1:], filler, item.dtype)
        return blank.at[run_targets].set(shaped)

    def unpack(base, arrived, slot_ids):
        flat = arrived.reshape((-1,) + arrived.shape[2:])
        return base.at[slot_ids.reshape(-1)].set(flat, mode="drop")

    arrived = (
        lax.all_to_all(pack(store[sources], 0), "group", split_axis=0, concat_axis=0, tiled=True),
        lax.all_to_all(pack(query[sources], 0), "group", split_axis=0, concat_axis=0, tiled=True),
        lax.all_to_all(
            pack(hidden_in[sources], 0), "group", split_axis=0, concat_axis=0, tiled=True
        ),
        lax.all_to_all(pack(lengths[sources], 0), "group", split_axis=0, concat_axis=0, tiled=True),
        lax.all_to_all(pack(places, slots), "group", split_axis=0, concat_axis=0, tiled=True),
    )
    slot_ids = arrived[4]
    store = unpack(store, arrived[0], slot_ids)
    query = unpack(query, arrived[1], slot_ids)
    source = unpack(hidden_in, arrived[2], slot_ids)
    counts = unpack(lengths, arrived[3], slot_ids)
    out_rows, fresh_rows = run_layers(
        source, query, store, counts, gain, kv_local, out_local, micro, columns, column_start
    )
    new_store = write_fresh(store, counts, fresh_rows)
    return (out_rows[None], new_store[None])


def solution(mesh):
    placed = (
        P("group", None),
        P("section", "group", "tensor"),
        P("section", "group", None, "tensor"),
        P("group"),
        P("group", None),
        P("section", None),
        P("section", None, "tensor"),
        P("section", "tensor", None),
    )
    return jax.shard_map(
        per_device,
        mesh=mesh,
        in_specs=placed,
        out_specs=(P("section", "group", "tensor"), P("section", "group", None, "tensor")),
        check_vma=False,
    )
```

profile of v0, /device:TPU:160, one launch (start us, length us, event | category | flops | bytes accessed | tf_op | source)
XLA Modules:
  0.0 735.1 jit_solution(4542038100115810150)
XLA Ops:
  9.3 1.7 copy.89
  14.5 4.2 all-to-all-start
  22.8 4.7 all-to-all-start.2
  28.1 1.9 scatter_fusion.3
  31.5 4.7 all-to-all-start.3
  38.6 2.0 scatter_fusion
  40.6 5.1 all-to-all-start.1
  47.2 2.2 scatter_fusion.5
  49.3 2.1 all-to-all-done.1
  51.4 5.1 all-to-all-start.4
  59.3 2.1 scatter_fusion.4
  62.3 2.4 scatter_fusion.1
  64.7 4.1 all-to-all-done.4
  68.8 2.1 scatter_fusion.6
  76.7 649.3 %while.21 = (s32[]{:T(128)}, bf16[32,4096]{1,0:T(8,128)(2,1)}, bf16[32,1024]{1,0:T(8,128)(2,1)}, bf16[32,256]{1,0:T(8,128)(2,1)}, pred[]{:T(512)}, /*index=5*/bf...) while((s32[]{:T(128)}, bf16[32,4096]{1,0:T(8,128)(2,1)}, ...), condition=%wide.wide.region_14.15_spmd.clone, body=%wide.wide.region_9.14_spmd.clone.sunk | while | flops 342064928 | bytes 18751428 | solution.py:104
  77.8 1.8 select_select_fusion.6
  84.9 5.6 convolution_convert_fusion.4
  90.5 50.3 %all-reduce.2.cloned.1.call-done = bf16[32,4096]{1,0:T(8,128)(2,1)} async-done(((bf16[32,4096]{1,0:T(8,128)(2,1)}), bf16[32,4096]{1,0:T(8,128)(2,1)}) %all-reduce.2.cloned.1.call-update) | async-done | bytes 262160 | tf_op jit(solution)/shard_map/while/body/eval_jaxpr/psum | solution.py:89
  140.9 1.7 fusion.76
  142.6 3.4 collective-permute-start
  147.5 14.7 %collective-permute-done = bf16[32,4096]{1,0:T(8,128)(2,1)S(1)} collective-permute-done((bf16[32,4096]{1,0:T(8,128)(2,1)}, bf16[32,4096]{1,0:T(8,128)(2,1)S(1)}, u32[]{:S(2)}, u32[]{:S(2)}) %collective-permute-start) | collective-permute-done | bytes 262176 | tf_op jit(solution)/shard_map/while/body/eval_jaxpr/ppermute | solution.py:13
  164.1 1.9 select_select_fusion.6
  171.2 5.6 convolution_convert_fusion.4
  176.8 44.5 %all-reduce.2.cloned.1.call-done = bf16[32,4096]{1,0:T(8,128)(2,1)} async-done(((bf16[32,4096]{1,0:T(8,128)(2,1)}), bf16[32,4096]{1,0:T(8,128)(2,1)}) %all-reduce.2.cloned.1.call-update) | async-done | bytes 262160 | tf_op jit(solution)/shard_map/while/body/eval_jaxpr/psum | solution.py:89
  221.3 1.7 fusion.76
  223.1 3.4 collective-permute-start
  228.0 14.7 %collective-permute-done = bf16[32,4096]{1,0:T(8,128)(2,1)S(1)} collective-permute-done((bf16[32,4096]{1,0:T(8,128)(2,1)}, bf16[32,4096]{1,0:T(8,128)(2,1)S(1)}, u32[]{:S(2)}, u32[]{:S(2)}) %collective-permute-start) | collective-permute-done | bytes 262176 | tf_op jit(solution)/shard_map/while/body/eval_jaxpr/ppermute | solution.py:13
  244.6 1.9 select_select_fusion.6
  251.6 5.6 convolution_convert_fusion.4
  257.3 44.5 %all-reduce.2.cloned.1.call-done = bf16[32,4096]{1,0:T(8,128)(2,1)} async-done(((bf16[32,4096]{1,0:T(8,128)(2,1)}), bf16[32,4096]{1,0:T(8,128)(2,1)}) %all-reduce.2.cloned.1.call-update) | async-done | bytes 262160 | tf_op jit(solution)/shard_map/while/body/eval_jaxpr/psum | solution.py:89
  301.8 1.7 fusion.76
  303.5 3.4 collective-permute-start
  308.4 14.7 %collective-permute-done = bf16[32,4096]{1,0:T(8,128)(2,1)S(1)} collective-permute-done((bf16[32,4096]{1,0:T(8,128)(2,1)}, bf16[32,4096]{1,0:T(8,128)(2,1)S(1)}, u32[]{:S(2)}, u32[]{:S(2)}) %collective-permute-start) | collective-permute-done | bytes 262176 | tf_op jit(solution)/shard_map/while/body/eval_jaxpr/ppermute | solution.py:13
  325.0 1.9 select_select_fusion.6
  332.1 5.6 convolution_convert_fusion.4
  337.7 44.5 %all-reduce.2.cloned.1.call-done = bf16[32,4096]{1,0:T(8,128)(2,1)} async-done(((bf16[32,4096]{1,0:T(8,128)(2,1)}), bf16[32,4096]{1,0:T(8,128)(2,1)}) %all-reduce.2.cloned.1.call-update) | async-done | bytes 262160 | tf_op jit(solution)/shard_map/while/body/eval_jaxpr/psum | solution.py:89
  382.2 1.7 fusion.76
  383.9 3.4 collective-permute-start
  388.8 14.7 %collective-permute-done = bf16[32,4096]{1,0:T(8,128)(2,1)S(1)} collective-permute-done((bf16[32,4096]{1,0:T(8,128)(2,1)}, bf16[32,4096]{1,0:T(8,128)(2,1)S(1)}, u32[]{:S(2)}, u32[]{:S(2)}) %collective-permute-start) | collective-permute-done | bytes 262176 | tf_op jit(solution)/shard_map/while/body/eval_jaxpr/ppermute | solution.py:13
  405.4 1.9 select_select_fusion.6
  412.5 5.6 convolution_convert_fusion.4
  418.2 44.5 %all-reduce.2.cloned.1.call-done = bf16[32,4096]{1,0:T(8,128)(2,1)} async-done(((bf16[32,4096]{1,0:T(8,128)(2,1)}), bf16[32,4096]{1,0:T(8,128)(2,1)}) %all-reduce.2.cloned.1.call-update) | async-done | bytes 262160 | tf_op jit(solution)/shard_map/while/body/eval_jaxpr/psum | solution.py:89
  462.6 1.7 fusion.76
  464.4 3.4 collective-permute-start
  469.3 14.7 %collective-permute-done = bf16[32,4096]{1,0:T(8,128)(2,1)S(1)} collective-permute-done((bf16[32,4096]{1,0:T(8,128)(2,1)}, bf16[32,4096]{1,0:T(8,128)(2,1)S(1)}, u32[]{:S(2)}, u32[]{:S(2)}) %collective-permute-start) | collective-permute-done | bytes 262176 | tf_op jit(solution)/shard_map/while/body/eval_jaxpr/ppermute | solution.py:13
  485.9 1.9 select_select_fusion.6
  492.9 5.6 convolution_convert_fusion.4
  498.6 44.5 %all-reduce.2.cloned.1.call-done = bf16[32,4096]{1,0:T(8,128)(2,1)} async-done(((bf16[32,4096]{1,0:T(8,128)(2,1)}), bf16[32,4096]{1,0:T(8,128)(2,1)}) %all-reduce.2.cloned.1.call-update) | async-done | bytes 262160 | tf_op jit(solution)/shard_map/while/body/eval_jaxpr/psum | solution.py:89
  543.1 1.7 fusion.76
  544.8 3.4 collective-permute-start
  549.7 14.7 %collective-permute-done = bf16[32,4096]{1,0:T(8,128)(2,1)S(1)} collective-permute-done((bf16[32,4096]{1,0:T(8,128)(2,1)}, bf16[32,4096]{1,0:T(8,128)(2,1)S(1)}, u32[]{:S(2)}, u32[]{:S(2)}) %collective-permute-start) | collective-permute-done | bytes 262176 | tf_op jit(solution)/shard_map/while/body/eval_jaxpr/ppermute | solution.py:13
  566.3 1.9 select_select_fusion.6
  573.4 5.6 convolution_convert_fusion.4
  579.0 44.5 %all-reduce.2.cloned.1.call-done = bf16[32,4096]{1,0:T(8,128)(2,1)} async-done(((bf16[32,4096]{1,0:T(8,128)(2,1)}), bf16[32,4096]{1,0:T(8,128)(2,1)}) %all-reduce.2.cloned.1.call-update) | async-done | bytes 262160 | tf_op jit(solution)/shard_map/while/body/eval_jaxpr/psum | solution.py:89
  623.5 1.7 fusion.76
  625.2 3.4 collective-permute-start
  630.1 14.7 %collective-permute-done = bf16[32,4096]{1,0:T(8,128)(2,1)S(1)} collective-permute-done((bf16[32,4096]{1,0:T(8,128)(2,1)}, bf16[32,4096]{1,0:T(8,128)(2,1)S(1)}, u32[]{:S(2)}, u32[]{:S(2)}) %collective-permute-start) | collective-permute-done | bytes 262176 | tf_op jit(solution)/shard_map/while/body/eval_jaxpr/ppermute | solution.py:13
  646.7 1.9 select_select_fusion.6
  653.8 5.6 convolution_convert_fusion.4
  659.5 44.5 %all-reduce.2.cloned.1.call-done = bf16[32,4096]{1,0:T(8,128)(2,1)} async-done(((bf16[32,4096]{1,0:T(8,128)(2,1)}), bf16[32,4096]{1,0:T(8,128)(2,1)}) %all-reduce.2.cloned.1.call-update) | async-done | bytes 262160 | tf_op jit(solution)/shard_map/while/body/eval_jaxpr/psum | solution.py:89
  703.9 1.7 fusion.76
  705.7 3.4 collective-permute-start
  710.6 14.7 %collective-permute-done = bf16[32,4096]{1,0:T(8,128)(2,1)S(1)} collective-permute-done((bf16[32,4096]{1,0:T(8,128)(2,1)}, bf16[32,4096]{1,0:T(8,128)(2,1)S(1)}, u32[]{:S(2)}, u32[]{:S(2)}) %collective-permute-start) | collective-permute-done | bytes 262176 | tf_op jit(solution)/shard_map/while/body/eval_jaxpr/ppermute | solution.py:13
  726.0 2.3 select_bitcast_fusion
  (196 shorter events, 93.5 us)
Async XLA Ops:
  12.2 64.5 %copy-start = (bf16[1,4096,256]{2,1,0:T(8,128)(2,1)S(1)}, bf16[1,4096,256]{2,1,0:T(8,128)(2,1)}, u32[]{:S(2)}) copy-start(bf16[1,4096,256]{2,1,0:T(8,128)(2,1)} %param.16) | copy-start | bytes 6291460
  14.5 8.3 %all-to-all-start = ((s32[8,1,2]{2,1,0:T(1,128)}), s32[8,1,2]{2,1,0:T(1,128)S(1)}, u32[]{:S(2)}, u32[]{:S(2)}) async-start(s32[8,1,2]{2,1,0:T(1,128)} %bitcast.20), calls=%async_computation | async-start | bytes 8192 | tf_op jit(solution)/shard_map/all_to_all | solution.py:139
  22.8 8.7 %all-to-all-start.2 = ((s32[8,1,2]{2,1,0:T(1,128)}), s32[8,1,2]{2,1,0:T(1,128)S(1)}, u32[]{:S(2)}, u32[]{:S(2)}) async-start(s32[8,1,2]{2,1,0:T(1,128)} %bitcast.21), calls=%async_computation.2 | async-start | bytes 8192 | tf_op jit(solution)/shard_map/all_to_all | solution.py:138
  31.5 9.1 %all-to-all-start.3 = ((bf16[8,2,1024]{2,1,0:T(2,128)(2,1)}), bf16[8,2,1024]{2,1,0:T(2,128)(2,1)S(1)}, u32[]{:S(2)}, u32[]{:S(2)}) async-start(bf16[8,2,1024]{2,1,0:T(2,128)(2,1)} %scatter_fusion.3), calls=%async_computation.3 | async-start | bytes 65536 | tf_op jit(solution)/shard_map/all_to_all | solution.py:134
  40.6 10.8 %all-to-all-start.1 = ((bf16[8,2,4096]{2,1,0:T(2,128)(2,1)}), bf16[8,2,4096]{2,1,0:T(2,128)(2,1)S(1)}, u32[]{:S(2)}, u32[]{:S(2)}) async-start(bf16[8,2,4096]{2,1,0:T(2,128)(2,1)} %scatter_fusion), calls=%async_computation.1 | async-start | bytes 262144 | tf_op jit(solution)/shard_map/all_to_all | solution.py:135
  51.4 17.4 %all-to-all-start.4 = ((bf16[8,2,64,256]{3,2,1,0:T(8,128)(2,1)}), bf16[8,2,64,256]{3,2,1,0:T(8,128)(2,1)}, u32[]{:S(2)}, u32[]{:S(2)}) async-start(bf16[8,2,64,256]{3,2,1,0:T(8,128)(2,1)} %scatter_fusion.5), calls=%async_computation.4 | async-start | bytes 1048576 | tf_op jit(solution)/shard_map/all_to_all | solution.py:133
  70.9 1.0 copy-start.1
  76.7 64.2 %all-reduce.2.cloned.1.call-start = ((), (), s32[]{:S(2)}) async-start(), calls=%async_computation.5 | async-start | bytes 524288 | tf_op jit(solution)/shard_map/while/body/eval_jaxpr/psum | solution.py:89
  142.6 19.6 %collective-permute-start = (bf16[32,4096]{1,0:T(8,128)(2,1)}, bf16[32,4096]{1,0:T(8,128)(2,1)S(1)}, u32[]{:S(2)}, u32[]{:S(2)}) collective-permute-start(bf16[32,4096]{1,0:T(8,128)(2,1)} %fusion.76), channel_id=1, source_target_pairs={{0,4},{4,8},{8,12},{12,16},{16,20},{20,24},{24,28},{1,5},{5,9},{9,... | collective-permute-start | bytes 786440 | tf_op jit(solution)/shard_map/while/body/eval_jaxpr/ppermute | solution.py:13
  162.3 0.7 copy-start.2
  163.0 58.4 %all-reduce.2.cloned.1.call-start = ((), (), s32[]{:S(2)}) async-start(), calls=%async_computation.5 | async-start | bytes 524288 | tf_op jit(solution)/shard_map/while/body/eval_jaxpr/psum | solution.py:89
  223.1 19.6 %collective-permute-start = (bf16[32,4096]{1,0:T(8,128)(2,1)}, bf16[32,4096]{1,0:T(8,128)(2,1)S(1)}, u32[]{:S(2)}, u32[]{:S(2)}) collective-permute-start(bf16[32,4096]{1,0:T(8,128)(2,1)} %fusion.76), channel_id=1, source_target_pairs={{0,4},{4,8},{8,12},{12,16},{16,20},{20,24},{24,28},{1,5},{5,9},{9,... | collective-permute-start | bytes 786440 | tf_op jit(solution)/shard_map/while/body/eval_jaxpr/ppermute | solution.py:13
  242.7 0.7 copy-start.2
  243.4 58.4 %all-reduce.2.cloned.1.call-start = ((), (), s32[]{:S(2)}) async-start(), calls=%async_computation.5 | async-start | bytes 524288 | tf_op jit(solution)/shard_map/while/body/eval_jaxpr/psum | solution.py:89
  303.5 19.6 %collective-permute-start = (bf16[32,4096]{1,0:T(8,128)(2,1)}, bf16[32,4096]{1,0:T(8,128)(2,1)S(1)}, u32[]{:S(2)}, u32[]{:S(2)}) collective-permute-start(bf16[32,4096]{1,0:T(8,128)(2,1)} %fusion.76), channel_id=1, source_target_pairs={{0,4},{4,8},{8,12},{12,16},{16,20},{20,24},{24,28},{1,5},{5,9},{9,... | collective-permute-start | bytes 786440 | tf_op jit(solution)/shard_map/while/body/eval_jaxpr/ppermute | solution.py:13
  323.1 0.7 copy-start.2
  323.8 58.4 %all-reduce.2.cloned.1.call-start = ((), (), s32[]{:S(2)}) async-start(), calls=%async_computation.5 | async-start | bytes 524288 | tf_op jit(solution)/shard_map/while/body/eval_jaxpr/psum | solution.py:89
  383.9 19.6 %collective-permute-start = (bf16[32,4096]{1,0:T(8,128)(2,1)}, bf16[32,4096]{1,0:T(8,128)(2,1)S(1)}, u32[]{:S(2)}, u32[]{:S(2)}) collective-permute-start(bf16[32,4096]{1,0:T(8,128)(2,1)} %fusion.76), channel_id=1, source_target_pairs={{0,4},{4,8},{8,12},{12,16},{16,20},{20,24},{24,28},{1,5},{5,9},{9,... | collective-permute-start | bytes 786440 | tf_op jit(solution)/shard_map/while/body/eval_jaxpr/ppermute | solution.py:13
  403.6 0.7 copy-start.2
  404.3 58.4 %all-reduce.2.cloned.1.call-start = ((), (), s32[]{:S(2)}) async-start(), calls=%async_computation.5 | async-start | bytes 524288 | tf_op jit(solution)/shard_map/while/body/eval_jaxpr/psum | solution.py:89
  464.4 19.6 %collective-permute-start = (bf16[32,4096]{1,0:T(8,128)(2,1)}, bf16[32,4096]{1,0:T(8,128)(2,1)S(1)}, u32[]{:S(2)}, u32[]{:S(2)}) collective-permute-start(bf16[32,4096]{1,0:T(8,128)(2,1)} %fusion.76), channel_id=1, source_target_pairs={{0,4},{4,8},{8,12},{12,16},{16,20},{20,24},{24,28},{1,5},{5,9},{9,... | collective-permute-start | bytes 786440 | tf_op jit(solution)/shard_map/while/body/eval_jaxpr/ppermute | solution.py:13
  484.0 0.7 copy-start.2
  484.7 58.4 %all-reduce.2.cloned.1.call-start = ((), (), s32[]{:S(2)}) async-start(), calls=%async_computation.5 | async-start | bytes 524288 | tf_op jit(solution)/shard_map/while/body/eval_jaxpr/psum | solution.py:89
  544.8 19.6 %collective-permute-start = (bf16[32,4096]{1,0:T(8,128)(2,1)}, bf16[32,4096]{1,0:T(8,128)(2,1)S(1)}, u32[]{:S(2)}, u32[]{:S(2)}) collective-permute-start(bf16[32,4096]{1,0:T(8,128)(2,1)} %fusion.76), channel_id=1, source_target_pairs={{0,4},{4,8},{8,12},{12,16},{16,20},{20,24},{24,28},{1,5},{5,9},{9,... | collective-permute-start | bytes 786440 | tf_op jit(solution)/shard_map/while/body/eval_jaxpr/ppermute | solution.py:13
  564.4 0.7 copy-start.2
  565.1 58.4 %all-reduce.2.cloned.1.call-start = ((), (), s32[]{:S(2)}) async-start(), calls=%async_computation.5 | async-start | bytes 524288 | tf_op jit(solution)/shard_map/while/body/eval_jaxpr/psum | solution.py:89
  625.2 19.6 %collective-permute-start = (bf16[32,4096]{1,0:T(8,128)(2,1)}, bf16[32,4096]{1,0:T(8,128)(2,1)S(1)}, u32[]{:S(2)}, u32[]{:S(2)}) collective-permute-start(bf16[32,4096]{1,0:T(8,128)(2,1)} %fusion.76), channel_id=1, source_target_pairs={{0,4},{4,8},{8,12},{12,16},{16,20},{20,24},{24,28},{1,5},{5,9},{9,... | collective-permute-start | bytes 786440 | tf_op jit(solution)/shard_map/while/body/eval_jaxpr/ppermute | solution.py:13
  644.9 0.7 copy-start.2
  645.6 58.4 %all-reduce.2.cloned.1.call-start = ((), (), s32[]{:S(2)}) async-start(), calls=%async_computation.5 | async-start | bytes 524288 | tf_op jit(solution)/shard_map/while/body/eval_jaxpr/psum | solution.py:89
  705.7 19.6 %collective-permute-start = (bf16[32,4096]{1,0:T(8,128)(2,1)}, bf16[32,4096]{1,0:T(8,128)(2,1)S(1)}, u32[]{:S(2)}, u32[]{:S(2)}) collective-permute-start(bf16[32,4096]{1,0:T(8,128)(2,1)} %fusion.76), channel_id=1, source_target_pairs={{0,4},{4,8},{8,12},{12,16},{16,20},{20,24},{24,28},{1,5},{5,9},{9,... | collective-permute-start | bytes 786440 | tf_op jit(solution)/shard_map/while/body/eval_jaxpr/ppermute | solution.py:13
  725.3 0.7 copy-start.2
Sparse Core Ops, SparseCore 0:
  90.7 50.1 all-reduce.1
  177.0 44.3 all-reduce.1
  257.4 44.3 all-reduce.1
  337.8 44.2 all-reduce.1
  418.3 44.3 all-reduce.1
  498.7 44.2 all-reduce.1
  579.1 44.3 all-reduce.1
  659.6 44.2 all-reduce.1
where the time goes:
time: 740 us; the launch traced here: 735 us
  waiting for transfers between devices  488 us (66%)
  local copies, waits for them, and re-layouts  66.2 us (9%)
  matrix products  65.4 us (9%)
  starting transfers between devices  50.8 us (7%)
  other arithmetic  49.9 us (7%)
  between operations  14.1 us (2%)
    psum x8, waiting for transfers between devices, advance(): lax.psum(partial_value.astype(jnp.bfloat16), 'tensor').astype(jnp.float32)  362 us
    ppermute x8, waiting for transfers between devices, passed_along(): return lax.ppermute(block, axis, route)  118 us
    dot_general x8, matrix products, decode_layer(): jnp.dot(context, out_weight, preferred_element_type=jnp.float32)  45.1 us
    ppermute x8, starting transfers between devices, passed_along(): return lax.ppermute(block, axis, route)  26.9 us
    dot_general x8, matrix products, decode_layer(): jnp.dot(normed, kv_weight, preferred_element_type=jnp.float32)  14.9 us
  transfers between devices with their start and end apart: 21, of which 20 were waited for; matrix products, arithmetic and copies ran while one was open for 5% of the time, Pallas kernels for 0%

commit v1 on v0

v1 whole, which is shorter than its diff:
```python
import functools

import jax
import jax.numpy as jnp
from jax import lax
from jax.experimental import pallas as pl
from jax.experimental.pallas import tpu as pltpu
from jax.sharding import PartitionSpec as P

HD = 128
PAIR = 2
ROWS = 16
HALVES = 2
MESH = pl.DeviceIdType.MESH
F32 = jnp.float32
BF16 = jnp.bfloat16
NONE = 255
LOW = -1e30


def iota(shape, axis):
    return lax.broadcasted_iota(jnp.int32, shape, axis)


def kernel(
    sizes,
    lens_in, moves_in, hidden, query, cache, gain, kvw, outw,
    xout_ref, fresh_out_ref, count_ref, base_v,
    lens_ref, moves_ref, xin, x0_v, q_v, qf_v, cache_v, gain_v, kvw_v, outw_v,
    mc_ref, sc_ref, ctx_ref, fresh_f, own_part, xnew, xnew_f, rs_send, rs_recv,
    pack, arr, info_pack, info_arr, place_v, place_s,
    perm_s, pick_ref, back_ref, sel_ref, sel2_ref, moved_ref, row_pack, row_arr,
    load_sem, outw_sem,
    rs_ss, rs_rs, ag_ss, ag_rs, hop_rs, fwd_ss, gc_ss, gc_rs, info_ss, info_rs, row_ss, row_rs,
    local_sem,
):
    G, L, T, micros, slots, width, ctx_len = sizes
    W = width // T
    H = HALVES
    S = W // H
    heads = W // HD
    pieces = heads + 2
    g = lax.axis_index("group")
    l = lax.axis_index("section")
    t = lax.axis_index("tensor")
    R = ROWS
    last = L - 1
    half = L // 2

    order = tuple(sorted(range(1, T), key=lambda d: -min(d, T - d)))

    def rs_copy(m, h, d):
        return pltpu.make_async_remote_copy(
            src_ref=rs_send.at[m, h, d - 1], dst_ref=rs_recv.at[m, h, d - 1],
            send_sem=rs_ss.at[m, h, d - 1], recv_sem=rs_rs.at[m, h],
            device_id={"tensor": lax.rem(t + d, T)}, device_id_type=MESH)

    def ag_copy(m, h, d):
        return pltpu.make_async_remote_copy(
            src_ref=xnew.at[m, h], dst_ref=xin.at[m, h, t],
            send_sem=ag_ss.at[m, h, d], recv_sem=ag_rs.at[m, h],
            device_id={"section": l + 1, "tensor": lax.rem(t + d, T)}, device_id_type=MESH)

    def hop_copy(m, h):
        return pltpu.make_async_remote_copy(
            src_ref=xnew.at[m, h], dst_ref=xin.at[m, h, t],
            send_sem=ag_ss.at[m, h, 0], recv_sem=hop_rs.at[m, h],
            device_id={"section": l + 1}, device_id_type=MESH)

    def fwd_copy(m, h, d):
        return pltpu.make_async_remote_copy(
            src_ref=xin.at[m, h, t], dst_ref=xin.at[m, h, t],
            send_sem=fwd_ss.at[m, h, d - 1], recv_sem=ag_rs.at[m, h],
            device_id={"tensor": lax.rem(t + d, T)}, device_id_type=MESH)

    def arrived(ref, sem):
        pltpu.make_async_copy(ref, ref, sem).wait()

    def to_group(src, dst, ss, rs, d):
        return pltpu.make_async_remote_copy(
            src_ref=src, dst_ref=dst, send_sem=ss.at[d - 1], recv_sem=rs.at[d - 1],
            device_id={"group": lax.rem(g + d, G)}, device_id_type=MESH)

    def gc_copy(d):
        e = PAIR * (d - 1)
        return to_group(pack.at[pl.ds(e, PAIR)], arr.at[pl.ds(e, PAIR)], gc_ss, gc_rs, d)

    def info_copy(d):
        return to_group(info_pack.at[d - 1], info_arr.at[d - 1], info_ss, info_rs, d)

    def row_copy(d):
        return to_group(row_pack.at[d - 1], row_arr.at[d - 1], row_ss, row_rs, d)

    def outw_load(h, d):
        start = pl.multiple_of(lax.rem(t + d, T) * W + h * S, S)
        place = order.index(d) if d else T - 1
        return pltpu.make_async_copy(
            outw.at[0, :, pl.ds(start, S)], outw_v.at[h, :, pl.ds(place * S, S)], outw_sem.at[h, d])

    query_load = pltpu.make_async_copy(query.at[0], q_v, load_sem.at[0])
    cache_load = pltpu.make_async_copy(cache.at[0], cache_v, load_sem.at[1])
    lens_load = pltpu.make_async_copy(lens_in, lens_ref, load_sem.at[5])
    moves_load = pltpu.make_async_copy(moves_in, moves_ref, load_sem.at[6])
    x_load = pltpu.make_async_copy(hidden, x0_v, load_sem.at[4])
    gain_load = pltpu.make_async_copy(gain, gain_v, load_sem.at[2])
    movers = moves_ref.shape[1]
    place_load = pltpu.make_async_copy(place_v.at[0], place_s, local_sem.at[0])

    lens_load.start()
    moves_load.start()
    query_load.start()
    cache_load.start()

    @pl.when(l == 0)
    def _():
        x_load.start()

    gain_load.start()
    for h in range(H):
        for q in range(T):
            pltpu.make_async_copy(
                kvw.at[0, pl.ds(q * W + h * S, S)], kvw_v.at[h, pl.ds(q * S, S)],
                load_sem.at[3]).start()

    for h in range(H):
        for d in order:
            outw_load(h, d).start()
    for h in range(H):
        outw_load(h, 0).start()

    barrier = pltpu.get_barrier_semaphore()
    for d in range(1, T):
        pl.semaphore_signal(barrier, inc=1, device_id={"tensor": lax.rem(t + d, T)}, device_id_type=MESH)
    for d in range(1, G):
        pl.semaphore_signal(barrier, inc=1, device_id={"group": lax.rem(g + d, G)}, device_id_type=MESH)

    @pl.when(l > 0)
    def _():
        for k in range(T):
            pl.semaphore_signal(
                barrier, inc=1, device_id={"section": l - 1, "tensor": k}, device_id_type=MESH)

    @pl.when((l > 0) & (l < last))
    def _():
        pl.semaphore_wait(barrier, T - 1 + G - 1 + T)

    @pl.when(l == last)
    def _():
        pl.semaphore_wait(barrier, T - 1 + G - 1)

    def arrange():
        leaving = [moves_ref[0, i] for i in range(movers)]
        ranked = list(leaving)
        for end in range(movers - 1, 0, -1):
            for i in range(end):
                low = jnp.minimum(ranked[i], ranked[i + 1])
                high = jnp.maximum(ranked[i], ranked[i + 1])
                ranked[i], ranked[i + 1] = low, high

        def staying(position):
            slot = position - movers
            for k in range(movers):
                slot = slot + (slot >= ranked[k]).astype(jnp.int32)
            return slot

        def slot_of(position):
            slot = staying(position)
            for i in range(movers):
                slot = jnp.where(position == i, leaving[i], slot)
            return slot

        def place(p, carry):
            perm_s[p] = staying(p)
            return carry

        for i in range(movers):
            perm_s[i] = leaving[i]
        lax.fori_loop(movers, slots, place, 0)
        square = (slots, slots)
        row, col = iota(square, 0), iota(square, 1)
        pick_ref[...] = jnp.where(slot_of(row) == col, 1.0, 0.0).astype(BF16)
        back_ref[...] = jnp.where((staying(col) == row) & (col >= movers), 1.0, 0.0).astype(BF16)

    block = 8
    blocks = slots // block

    def attend(first, end):
        span = block * ctx_len
        scale = HD ** -0.5

        def one(b, carry):
            rows = pl.ds(pl.multiple_of(b * block, block), block)
            lens = jnp.zeros((block, span), jnp.int32)
            row = iota((block, span), 0)
            slot = [perm_s[b * block + n] for n in range(block)]
            for n in range(block):
                lens = jnp.where(row == n, lens_ref[slot[n]], lens)
            tokens = jnp.concatenate([cache_v[slot[n]] for n in range(block)], axis=0)
            col = iota((block, span), 1)
            ok = (col // ctx_len == row) & (col % ctx_len < lens)
            bias = jnp.where(ok, 0.0, LOW).astype(F32)
            stacked = jnp.concatenate(
                [qf_v[rows, a * HD:(a + 1) * HD] for a in range(heads)], axis=0).astype(BF16)
            keys = tokens[:, 0:HD]
            values = tokens[:, HD:2 * HD]
            score = lax.dot_general(
                stacked, keys, (((1,), (1,)), ((), ())), preferred_element_type=F32)
            score = score.reshape(heads, block, span) * scale + bias[None]
            top = jnp.max(score, axis=-1, keepdims=True)
            weight = jnp.exp(score - top)
            total = jnp.sum(weight, axis=-1, keepdims=True)
            mixed = jnp.dot(
                weight.reshape(heads * block, span).astype(BF16), values,
                preferred_element_type=F32)
            ctx_ref[:, rows, :] = mixed.reshape(heads, block, HD)
            mc_ref[:, rows, :] = jnp.broadcast_to(top, (heads, block, HD))
            sc_ref[:, rows, :] = jnp.broadcast_to(total, (heads, block, HD))
            return carry

        lax.fori_loop(first, end, one, 0)

    def depart():
        lane = iota((8, 256), 1)
        sel_row = iota(sel_ref.shape, 0)
        slot_at = jnp.full(sel_ref.shape, NONE, jnp.int32)
        for d in range(1, G):
            e = d - 1
            dest = lax.rem(g + d, G)
            place_vec = jnp.zeros((8, 256), jnp.int32)
            len_vec = jnp.zeros((8, 256), jnp.int32)
            for i in range(PAIR):
                slot = jnp.int32(NONE)
                place = jnp.int32(NONE)
                from_slot = jnp.int32(0)
                for k in range(movers // PAIR):
                    hit = moves_ref[1, PAIR * k] == dest
                    slot = jnp.where(hit, PAIR * k + i, slot)
                    place = jnp.where(hit, moves_ref[2, PAIR * k + i], place)
                    from_slot = jnp.where(hit, moves_ref[0, PAIR * k + i], from_slot)
                here = lane // 16 == e * PAIR + i
                place_vec = jnp.where(here, place, place_vec)
                len_vec = jnp.where(here, lens_ref[from_slot], len_vec)
                slot_at = jnp.where(sel_row // 16 == e * PAIR + i, slot, slot_at)
                pack[PAIR * e + i] = cache_v[from_slot]
            info_pack[e, 0:8, :] = place_vec
            info_pack[e, 8:16, :] = len_vec
            info_copy(d).start()
            gc_copy(d).start()
        sel_col = iota(sel_ref.shape, 1)
        chosen = (sel_row % 16 == sel_col // R) & (slot_at == sel_col % R)
        sel_ref[...] = jnp.where(chosen, 1.0, 0.0).astype(BF16)

    def arrive():
        for d in range(1, G):
            info_copy(d).wait_recv()
        place = info_arr[0, 0:8, :]
        length = info_arr[0, 8:16, :]
        for e in range(1, G - 1):
            place = place + info_arr[e, 0:8, :]
            length = length + info_arr[e, 8:16, :]
        lane8 = iota((8, 256), 1)
        place = jnp.where(lane8 < (G - 1) * PAIR * 16, place, NONE)
        place_v[0] = place
        place_load.start()
        wide = (slots, 256)
        spot = jnp.broadcast_to(place[0:1, :], wide)
        long = jnp.broadcast_to(length[0:1, :], wide)
        lane = iota(wide, 1)
        row = iota(wide, 0)
        match = spot == row
        first = match & (lane % 16 == 0)
        has = jnp.max(jnp.where(first, 1.0, 0.0), axis=-1, keepdims=True)
        moved_len = jnp.max(jnp.where(first, long.astype(F32), 0.0), axis=-1, keepdims=True)
        own_len = jnp.zeros((slots, HD), F32)
        narrow = iota((slots, HD), 0)
        for n in range(slots):
            own_len = jnp.where(narrow == n, lens_ref[n].astype(F32), own_len)
        count_ref[...] = jnp.where(has > 0.5, moved_len, own_len).astype(jnp.int32)
        for c in range(pieces):
            sel2_ref[c * slots:(c + 1) * slots, :] = jnp.where(
                match & (lane % 16 == c), 1.0, 0.0).astype(BF16)
        for d in range(1, G):
            gc_copy(d).wait_recv()
        place_load.wait()

        def fill(j, carry):
            index = jnp.int32(-1)
            for e in range((G - 1) * PAIR):
                index = jnp.where(place_s[0, e * 16] == j, e, index)
            moved = arr[jnp.maximum(index, 0)]
            kept = cache_v[j]
            base_v[j] = lax.select_n(index >= 0, kept, moved)
            return carry

        lax.fori_loop(0, slots, fill, 0)

    def pass_on(m, h):
        arrived(xin.at[m, h, t], hop_rs.at[m, h])
        for d in order:
            fwd_copy(m, h, d).start()

    def forward(m):
        @pl.when(l == half)
        def _():
            for h in range(H):
                pass_on(m, h)

    def whole_fresh():
        acc = jnp.zeros((slots, 2 * HD), F32)
        square = jnp.zeros((slots, 1), F32)
        for h in range(H):
            scaled = []
            for q in range(T):
                cols = slice(q * W + h * S, q * W + (h + 1) * S)
                xq = x0_v[:, cols].astype(F32)
                square = square + jnp.sum(xq * xq, axis=-1, keepdims=True)
                scaled.append((xq * gain_v[:, cols]).astype(BF16))
            acc = acc + jnp.dot(
                jnp.concatenate(scaled, axis=1), kvw_v[h], preferred_element_type=F32)
        fresh = (acc * lax.rsqrt(square * (1.0 / width) + 1e-06)).astype(BF16)
        fresh_f[...] = jnp.dot(pick_ref[...], fresh, preferred_element_type=F32)
        mine = x0_v[:, pl.ds(pl.multiple_of(t * W, W), W)]
        ordered = jnp.dot(pick_ref[...], mine, preferred_element_type=F32).astype(BF16)
        for m in range(micros):
            for h in range(H):
                xin[m, h, t] = ordered[m * R:(m + 1) * R, h * S:(h + 1) * S]

    def fresh_part(m):
        rows = pl.ds(pl.multiple_of(m * R, R), R)
        acc = jnp.zeros((R, 2 * HD), F32)
        square = jnp.zeros((R, 1), F32)
        for h in range(H):

            @pl.when(l != half)
            def _():
                arrived(xin.at[m, h], ag_rs.at[m, h])

            @pl.when(l == half)
            def _():
                arrived(xin.at[m, h, pl.ds(0, T - 1)], ag_rs.at[m, h])

            scaled = []
            for q in range(T):
                cols = slice(q * W + h * S, q * W + (h + 1) * S)
                xq = xin[m, h, q].astype(F32)
                square = square + jnp.sum(xq * xq, axis=-1, keepdims=True)
                scaled.append((xq * gain_v[:, cols]).astype(BF16))
            acc = acc + jnp.dot(
                jnp.concatenate(scaled, axis=1), kvw_v[h], preferred_element_type=F32)
        fresh = (acc * lax.rsqrt(square * (1.0 / width) + 1e-06)).astype(BF16).astype(F32)
        fresh_f[rows, :] = fresh

    def front(m):
        rows = pl.ds(pl.multiple_of(m * R, R), R)

        @pl.when(l > 0)
        def _():
            fresh_part(m)

        fresh = fresh_f[rows, :]
        key = fresh[:, 0:HD]
        value = fresh[:, HD:2 * HD]
        parts = []
        for a in range(heads):
            qa = qf_v[rows, a * HD:(a + 1) * HD]
            own = jnp.sum(qa * key, axis=-1, keepdims=True) * (HD ** -0.5)
            old_top = mc_ref[a, rows, :]
            top = jnp.maximum(old_top, own)
            old_scale = jnp.exp(old_top - top)
            own_weight = jnp.exp(own - top)
            total = sc_ref[a, rows, :] * old_scale + own_weight
            mixed = (ctx_ref[a, rows, :] * old_scale + own_weight * value) / total
            parts.append(mixed.astype(BF16))
        return jnp.concatenate(parts, axis=1)

    def project(m, context, h):
        for i, d in enumerate(order):
            part = jnp.dot(
                context, outw_v[h, :, i * S:(i + 1) * S], preferred_element_type=F32)
            rs_send[m, h, d - 1] = part.astype(BF16)
            rs_copy(m, h, d).start()

    def project_own(m, context, h):
        own_part[m, h] = jnp.dot(
            context, outw_v[h, :, (T - 1) * S:T * S], preferred_element_type=F32)

    def reduce(m, h):
        total = own_part[m, h] + xin[m, h, t].astype(F32)
        arrived(rs_recv.at[m, h], rs_rs.at[m, h])
        for d in order:
            total = total + rs_recv[m, h, d - 1].astype(F32)
        rounded = total.astype(BF16)
        xnew[m, h] = rounded
        xnew_f[pl.ds(pl.multiple_of(m * R, R), R), h * S:(h + 1) * S] = rounded.astype(F32)

        @pl.when((l < last) & (l != half - 1))
        def _():
            for d in order + (0,):
                ag_copy(m, h, d).start()

        @pl.when(l == half - 1)
        def _():
            hop_copy(m, h).start()

    def exchange():
        stacked = jnp.concatenate(
            [xnew_f[0:R, c * HD:(c + 1) * HD] for c in range(heads)]
            + [fresh_f[0:R, c * HD:(c + 1) * HD] for c in range(2)], axis=0).astype(BF16)
        leaving = jnp.dot(sel_ref[...], stacked, preferred_element_type=F32).astype(BF16)
        for d in range(1, G):
            row_pack[d - 1] = leaving[(d - 1) * 32:d * 32]
            row_copy(d).start()

    def collect():
        row_arr[G - 1] = jnp.zeros((32, HD), BF16)
        for d in range(1, G):
            row_copy(d).wait_recv()
        moved_ref[...] = jnp.dot(
            sel2_ref[...], row_arr[...].reshape(G * 32, HD), preferred_element_type=F32)

    lens_load.wait()
    moves_load.wait()
    arrange()
    query_load.wait()
    cache_load.wait()
    qf_v[...] = jnp.dot(pick_ref[...], q_v[...], preferred_element_type=F32)
    first = R // block
    attend(0, first)

    @pl.when(l > 0)
    def _():
        attend(first, blocks)
        depart()

    @pl.when(l == 0)
    def _():
        x_load.wait()
        gain_load.wait()
        arrived(kvw_v, load_sem.at[3])
        whole_fresh()

    @pl.when(l >= 3)
    def _():
        arrive()

    @pl.when(l > 0)
    def _():
        gain_load.wait()
        arrived(kvw_v, load_sem.at[3])

    forward(0)

    def batch(m, carry):
        context = front(m)

        @pl.when((l == 0) & (m == 0))
        def _():
            pl.semaphore_wait(barrier, T - 1 + G - 1 + T)

        @pl.when(m == 0)
        def _():
            for h in range(H):
                for d in order + (0,):
                    outw_load(h, d).wait()

        for h in range(H):
            project(m, context, h)

        @pl.when(m + 1 < micros)
        def _():
            forward(m + 1)

        for h in range(H):
            project_own(m, context, h)

        @pl.when((l == 0) & (m == 0))
        def _():
            attend(first, blocks)

        @pl.when((l == last) & (m == micros - 1))
        def _():
            collect()

        for h in range(H):
            reduce(m, h)

        @pl.when((l == last) & (m == 0))
        def _():
            exchange()

        return carry

    lax.fori_loop(0, micros, batch, 0)

    @pl.when(l == 0)
    def _():
        depart()

    @pl.when(l < 3)
    def _():
        arrive()

    @pl.when(l < last)
    def _():
        exchange()
        collect()

    back = back_ref[...]
    for c in range(pieces):
        piece = (xnew_f[:, c * HD:(c + 1) * HD] if c < heads
                 else fresh_f[:, (c - heads) * HD:(c - heads + 1) * HD])
        kept = jnp.dot(back, piece.astype(BF16), preferred_element_type=F32)
        result = (kept + moved_ref[c * slots:(c + 1) * slots, :]).astype(BF16)
        if c < heads:
            xout_ref[:, c * HD:(c + 1) * HD] = result
        else:
            fresh_out_ref[:, (c - heads) * HD:(c - heads + 1) * HD] = result

    for m in range(micros):
        for h in range(H):
            for d in order:
                rs_copy(m, h, d).wait_send()
    for d in range(1, G):
        info_copy(d).wait_send()
        gc_copy(d).wait_send()
        row_copy(d).wait_send()

    @pl.when((l < last) & (l != half - 1))
    def _():
        for m in range(micros):
            for h in range(H):
                for d in range(T):
                    ag_copy(m, h, d).wait_send()

    @pl.when(l == half - 1)
    def _():
        for m in range(micros):
            for h in range(H):
                hop_copy(m, h).wait_send()

    @pl.when(l == half)
    def _():
        for m in range(micros):
            for h in range(H):
                for d in order:
                    fwd_copy(m, h, d).wait_send()


def finish(chunks, xout, fresh_ref, count_ref, base, layer_out, new_cache, held, out_sem, x_sem):
    slots, ctx_len, kv = held.shape
    part = slots // chunks

    def store(c):
        rows = pl.ds(c * part, part)
        return pltpu.make_async_copy(held.at[rows], new_cache.at[0, rows], out_sem.at[c])

    rows_copy = pltpu.make_async_copy(xout, layer_out.at[0], x_sem.at[0])
    rows_copy.start()
    token = iota((ctx_len, HD), 0)
    for c in range(chunks):
        for j in range(c * part, (c + 1) * part):
            here = token == count_ref[j:j + 1, :]
            for k in range(kv // HD):
                cols = slice(k * HD, (k + 1) * HD)
                row = fresh_ref[j:j + 1, cols].astype(F32)
                held[j, :, cols] = jnp.where(here, row, base[j, :, cols].astype(F32)).astype(BF16)
        store(c).start()
    rows_copy.wait()
    for c in range(chunks):
        store(c).wait()


def per_device(sizes, hidden_in, queries, cache, lengths, moves, norm_gain, kv_weight, out_weight):
    G, L, T, micros, slots, width, ctx_len = sizes
    W = width // T
    heads = W // HD
    pieces = heads + 2
    R = ROWS
    H = HALVES
    S = W // H
    kv = 2 * HD
    movers = (G - 1) * PAIR
    any_spec = pl.BlockSpec(memory_space=pl.ANY)
    vmem = pl.BlockSpec(memory_space=pltpu.VMEM)
    dma = pltpu.SemaphoreType.DMA
    xout, fresh, count, base = pl.pallas_call(
        functools.partial(kernel, sizes),
        out_shape=(
            pltpu.VMEM((slots, W), BF16),
            pltpu.VMEM((slots, kv), BF16),
            pltpu.VMEM((slots, HD), jnp.int32),
            pltpu.VMEM((slots, ctx_len, kv), BF16),
        ),
        in_specs=[any_spec] * 8,
        out_specs=(vmem, vmem, vmem, vmem),
        scratch_shapes=[
            pltpu.SMEM(lengths.shape, jnp.int32),
            pltpu.SMEM(moves.shape[::-1], jnp.int32),
            pltpu.VMEM((micros, H, T, R, S), BF16),
            pltpu.VMEM((slots, width), BF16),
            pltpu.VMEM((slots, W), BF16),
            pltpu.VMEM((slots, W), F32),
            pltpu.VMEM((slots, ctx_len, kv), BF16),
            pltpu.VMEM((1, width), F32),
            pltpu.VMEM((H, T * S, kv), BF16),
            pltpu.VMEM((H, W, T * S), BF16),
            pltpu.VMEM((heads, slots, HD), F32),
            pltpu.VMEM((heads, slots, HD), F32),
            pltpu.VMEM((heads, slots, HD), F32),
            pltpu.VMEM((slots, kv), F32),
            pltpu.VMEM((micros, H, R, S), F32),
            pltpu.VMEM((micros, H, R, S), BF16),
            pltpu.VMEM((slots, W), F32),
            pltpu.VMEM((micros, H, T - 1, R, S), BF16),
            pltpu.VMEM((micros, H, T - 1, R, S), BF16),
            pltpu.VMEM((movers, ctx_len, kv), BF16),
            pltpu.VMEM((movers, ctx_len, kv), BF16),
            pltpu.VMEM((G - 1, 16, 256), jnp.int32),
            pltpu.VMEM((G - 1, 16, 256), jnp.int32),
            pltpu.VMEM((1, 8, 256), jnp.int32),
            pltpu.SMEM((8, 256), jnp.int32),
            pltpu.SMEM((slots,), jnp.int32),
            pltpu.VMEM((slots, slots), BF16),
            pltpu.VMEM((slots, slots), BF16),
            pltpu.VMEM(((G - 1) * 32, pieces * R), BF16),
            pltpu.VMEM((pieces * slots, 256), BF16),
            pltpu.VMEM((pieces * slots, HD), F32),
            pltpu.VMEM((G - 1, 32, HD), BF16),
            pltpu.VMEM((G, 32, HD), BF16),
            dma((7,)), dma((H, T)),
            dma((micros, H, T - 1)), dma((micros, H)),
            dma((micros, H, T)), dma((micros, H)), dma((micros, H)), dma((micros, H, T - 1)),
            dma((G - 1,)), dma((G - 1,)), dma((G - 1,)), dma((G - 1,)), dma((G - 1,)), dma((G - 1,)),
            dma((1,)),
        ],
        compiler_params=pltpu.CompilerParams(
            collective_id=0, has_side_effects=True, vmem_limit_bytes=56 * 1024 * 1024),
        name="chain",
    )(lengths, moves.T, hidden_in, queries, cache, norm_gain, kv_weight, out_weight)
    chunks = 4
    return pl.pallas_call(
        functools.partial(finish, chunks),
        out_shape=(
            jax.ShapeDtypeStruct((1, slots, W), BF16),
            jax.ShapeDtypeStruct((1, slots, ctx_len, kv), BF16),
        ),
        in_specs=[vmem] * 4,
        out_specs=(any_spec, any_spec),
        scratch_shapes=[pltpu.VMEM((slots, ctx_len, kv), BF16), dma((chunks,)), dma((1,))],
        compiler_params=pltpu.CompilerParams(vmem_limit_bytes=16 * 1024 * 1024),
        name="finish",
    )(*(pltpu.with_memory_space_constraint(part, pltpu.VMEM) for part in (xout, fresh, count, base)))


def solution(mesh):
    G, L, T = mesh.shape["group"], mesh.shape["section"], mesh.shape["tensor"]

    def whole(hidden_in, queries, cache, lengths, moves, norm_gain, kv_weight, out_weight):
        slots = hidden_in.shape[0] // G
        sizes = (G, L, T, slots // ROWS, slots, hidden_in.shape[1], cache.shape[2])
        return jax.shard_map(
            functools.partial(per_device, sizes),
            mesh=mesh,
            in_specs=(
                P("group", None),
                P("section", "group", "tensor"),
                P("section", "group", None, "tensor"),
                P("group"),
                P("group", None),
                P("section", None),
                P("section", None, "tensor"),
                P("section", "tensor", None),
            ),
            out_specs=(P("section", "group", "tensor"), P("section", "group", None, "tensor")),
            check_vma=False,
        )(hidden_in, queries, cache, lengths, moves, norm_gain, kv_weight, out_weight)

    return whole
```

time: 740 us -> 90.8 us (0.12)
  the two profiles are of different devices: /device:TPU:160 before, /device:TPU:230 now
where the time goes in v1:
time: 90.8 us; the launch traced here: 90.7 us
  Pallas kernels  90 us (99%)
    pallas_call x1, Pallas kernels, per_device(): pl.pallas_call(functools.partial(kernel, sizes), out_shape=(pltpu.VMEM((s...  89 us

profile of v1, /device:TPU:230, one launch (start us, length us, event | category | flops | bytes accessed | tf_op | source)
XLA Modules:
  0.0 90.7 jit_solution(1517937764312321920)
XLA Ops:
  0.6 89.0 %chain.1 = (bf16[32,1024]{1,0:T(8,128)(2,1)S(1)}, bf16[32,256]{1,0:T(8,128)(2,1)S(1)}, s32[32,128]{1,0:T(8,128)S(1)}, bf16[32,64,256]{2,1,0:T(8,128)(2,1)S(1)}) custom-call(s32[32]{0:T(128)} %lens_in.1, s32[3,6]{1,0:T(4,128)} %bitcast.1, bf16[32,4096]{1,0:T(8,128)(2,1)} %hidden.1, bf16[1,32,1024]{2,1,0:T(8,128)(2,1)} %query.1, ...), custom_call_target="tpu_custom_call" | custom-call | tf_op jit(solution)/shard_map/chain/pallas_call | solution.py:586
  89.6 1.1 %finish.1 = (bf16[1,32,1024]{2,1,0:T(8,128)(2,1)}, bf16[1,32,64,256]{3,2,1,0:T(8,128)(2,1)}) custom-call(bf16[32,1024]{1,0:T(8,128)(2,1)S(1)} %get-tuple-element.6.xout, bf16[32,256]{1,0:T(8,128)(2,1)S(1)} %get-tuple-element.7.fresh_ref, s32[32,128]{1,0:T(8,128)S(1)} %get-tuple-element.8.count_ref, bf16[32,64,256]{2,1,0:T(8,128)(2,1)S(1)} %get-tuple-element.9.base), custom_call_target="tpu_custom_call" | custom-call | tf_op jit(solution)/shard_map/finish/pallas_call | solution.py:641

commit v2 on v1

--- a/solution.py
+++ b/solution.py
@@ -25,8 +25,8 @@
 def kernel(
     sizes,
     lens_in, moves_in, hidden, query, cache, gain, kvw, outw,
-    xout_ref, fresh_out_ref, count_ref, base_v,
-    lens_ref, moves_ref, xin, x0_v, q_v, qf_v, cache_v, gain_v, kvw_v, outw_v,
+    xout_ref, base_v,
+    count_ref, lens_ref, moves_ref, xin, x0_v, q_v, qf_v, cache_v, gain_v, kvw_v, outw_v,
     mc_ref, sc_ref, ctx_ref, fresh_f, own_part, xnew, xnew_f, rs_send, rs_recv,
     pack, arr, info_pack, info_arr, place_v, place_s,
     perm_s, pick_ref, back_ref, sel_ref, sel2_ref, moved_ref, row_pack, row_arr,
@@ -302,8 +302,7 @@
     def forward(m):
         @pl.when(l == half)
         def _():
-            for h in range(H):
-                pass_on(m, h)
+            pass_on(m, 0)
 
     def whole_fresh():
         acc = jnp.zeros((slots, 2 * HD), F32)
@@ -331,13 +330,17 @@
         square = jnp.zeros((R, 1), F32)
         for h in range(H):
 
-            @pl.when(l != half)
-            def _():
+            if h:
                 arrived(xin.at[m, h], ag_rs.at[m, h])
-
-            @pl.when(l == half)
-            def _():
-                arrived(xin.at[m, h, pl.ds(0, T - 1)], ag_rs.at[m, h])
+            else:
+
+                @pl.when(l != half)
+                def _():
+                    arrived(xin.at[m, h], ag_rs.at[m, h])
+
+                @pl.when(l == half)
+                def _():
+                    arrived(xin.at[m, h, pl.ds(0, T - 1)], ag_rs.at[m, h])
 
             scaled = []
             for q in range(T):
@@ -377,8 +380,11 @@
         for i, d in enumerate(order):
             part = jnp.dot(
                 context, outw_v[h, :, i * S:(i + 1) * S], preferred_element_type=F32)
+            if i or h:
+                rs_copy(m, h if i else h - 1, order[i - 1]).start()
             rs_send[m, h, d - 1] = part.astype(BF16)
-            rs_copy(m, h, d).start()
+        if h == H - 1:
+            rs_copy(m, h, order[-1]).start()
 
     def project_own(m, context, h):
         own_part[m, h] = jnp.dot(
@@ -393,14 +399,16 @@
         xnew[m, h] = rounded
         xnew_f[pl.ds(pl.multiple_of(m * R, R), R), h * S:(h + 1) * S] = rounded.astype(F32)
 
-        @pl.when((l < last) & (l != half - 1))
+        @pl.when((l < last) if h else (l < last) & (l != half - 1))
         def _():
             for d in order + (0,):
                 ag_copy(m, h, d).start()
 
-        @pl.when(l == half - 1)
-        def _():
-            hop_copy(m, h).start()
+        if h == 0:
+
+            @pl.when(l == half - 1)
+            def _():
+                hop_copy(m, h).start()
 
     def exchange():
         stacked = jnp.concatenate(
@@ -418,6 +426,18 @@
         moved_ref[...] = jnp.dot(
             sel2_ref[...], row_arr[...].reshape(G * 32, HD), preferred_element_type=F32)
 
+    def settle():
+        kept = jnp.dot(back_ref[...], fresh_f[...].astype(BF16), preferred_element_type=F32)
+        token = iota((ctx_len, HD), 0)
+        for k in range(2):
+            cols = slice(k * HD, (k + 1) * HD)
+            c = heads + k
+            fresh = kept[:, cols] + moved_ref[c * slots:(c + 1) * slots, :]
+            for j in range(slots):
+                here = token == count_ref[j:j + 1, :]
+                base_v[j, :, cols] = jnp.where(
+                    here, fresh[j:j + 1, :], base_v[j, :, cols].astype(F32)).astype(BF16)
+
     lens_load.wait()
     moves_load.wait()
     arrange()
@@ -480,6 +500,7 @@
         @pl.when((l == last) & (m == micros - 1))
         def _():
             collect()
+            settle()
 
         for h in range(H):
             reduce(m, h)
@@ -504,17 +525,12 @@
     def _():
         exchange()
         collect()
-
-    back = back_ref[...]
-    for c in range(pieces):
-        piece = (xnew_f[:, c * HD:(c + 1) * HD] if c < heads
-                 else fresh_f[:, (c - heads) * HD:(c - heads + 1) * HD])
-        kept = jnp.dot(back, piece.astype(BF16), preferred_element_type=F32)
-        result = (kept + moved_ref[c * slots:(c + 1) * slots, :]).astype(BF16)
-        if c < heads:
-            xout_ref[:, c * HD:(c + 1) * HD] = result
-        else:
-            fresh_out_ref[:, (c - heads) * HD:(c - heads + 1) * HD] = result
+        settle()
+
+    kept = jnp.dot(back_ref[...], xnew_f[...].astype(BF16), preferred_element_type=F32)
+    for c in range(heads):
+        cols = slice(c * HD, (c + 1) * HD)
+        xout_ref[:, cols] = (kept[:, cols] + moved_ref[c * slots:(c + 1) * slots, :]).astype(BF16)
 
     for m in range(micros):
         for h in range(H):
@@ -528,46 +544,42 @@
     @pl.when((l < last) & (l != half - 1))
     def _():
         for m in range(micros):
-            for h in range(H):
+            for d in range(T):
+                ag_copy(m, 0, d).wait_send()
+
+    @pl.when(l < last)
+    def _():
+        for m in range(micros):
+            for h in range(1, H):
                 for d in range(T):
                     ag_copy(m, h, d).wait_send()
 
     @pl.when(l == half - 1)
     def _():
         for m in range(micros):
-            for h in range(H):
-                hop_copy(m, h).wait_send()
+            hop_copy(m, 0).wait_send()
 
     @pl.when(l == half)
     def _():
         for m in range(micros):
-            for h in range(H):
-                for d in order:
-                    fwd_copy(m, h, d).wait_send()
-
-
-def finish(chunks, xout, fresh_ref, count_ref, base, layer_out, new_cache, held, out_sem, x_sem):
-    slots, ctx_len, kv = held.shape
-    part = slots // chunks
+            for d in order:
+                fwd_copy(m, 0, d).wait_send()
+
+
+def finish(chunks, xout, base, layer_out, new_cache, out_sem, x_sem):
+    part = base.shape[0] // chunks
 
     def store(c):
         rows = pl.ds(c * part, part)
-        return pltpu.make_async_copy(held.at[rows], new_cache.at[0, rows], out_sem.at[c])
+        return pltpu.make_async_copy(base.at[rows], new_cache.at[0, rows], out_sem.at[c])
 
     rows_copy = pltpu.make_async_copy(xout, layer_out.at[0], x_sem.at[0])
+    for c in range(chunks):
+        store(c).start()
     rows_copy.start()
-    token = iota((ctx_len, HD), 0)
-    for c in range(chunks):
-        for j in range(c * part, (c + 1) * part):
-            here = token == count_ref[j:j + 1, :]
-            for k in range(kv // HD):
-                cols = slice(k * HD, (k + 1) * HD)
-                row = fresh_ref[j:j + 1, cols].astype(F32)
-                held[j, :, cols] = jnp.where(here, row, base[j, :, cols].astype(F32)).astype(BF16)
-        store(c).start()
-    rows_copy.wait()
     for c in range(chunks):
         store(c).wait()
+    rows_copy.wait()
 
 
 def per_device(sizes, hidden_in, queries, cache, lengths, moves, norm_gain, kv_weight, out_weight):
@@ -583,17 +595,16 @@
     any_spec = pl.BlockSpec(memory_space=pl.ANY)
     vmem = pl.BlockSpec(memory_space=pltpu.VMEM)
     dma = pltpu.SemaphoreType.DMA
-    xout, fresh, count, base = pl.pallas_call(
+    xout, base = pl.pallas_call(
         functools.partial(kernel, sizes),
         out_shape=(
             pltpu.VMEM((slots, W), BF16),
-            pltpu.VMEM((slots, kv), BF16),
-            pltpu.VMEM((slots, HD), jnp.int32),
             pltpu.VMEM((slots, ctx_len, kv), BF16),
         ),
         in_specs=[any_spec] * 8,
-        out_specs=(vmem, vmem, vmem, vmem),
+        out_specs=(vmem, vmem),
         scratch_shapes=[
+            pltpu.VMEM((slots, HD), jnp.int32),
             pltpu.SMEM(lengths.shape, jnp.int32),
             pltpu.SMEM(moves.shape[::-1], jnp.int32),
             pltpu.VMEM((micros, H, T, R, S), BF16),
@@ -644,12 +655,12 @@
             jax.ShapeDtypeStruct((1, slots, W), BF16),
             jax.ShapeDtypeStruct((1, slots, ctx_len, kv), BF16),
         ),
-        in_specs=[vmem] * 4,
+        in_specs=[vmem] * 2,
         out_specs=(any_spec, any_spec),
-        scratch_shapes=[pltpu.VMEM((slots, ctx_len, kv), BF16), dma((chunks,)), dma((1,))],
+        scratch_shapes=[dma((chunks,)), dma((1,))],
         compiler_params=pltpu.CompilerParams(vmem_limit_bytes=16 * 1024 * 1024),
         name="finish",
-    )(*(pltpu.with_memory_space_constraint(part, pltpu.VMEM) for part in (xout, fresh, count, base)))
+    )(*(pltpu.with_memory_space_constraint(part, pltpu.VMEM) for part in (xout, base)))
 
 
 def solution(mesh):

time: 90.8 us -> 88.9 us (0.979)
  Pallas kernels: 90 us -> 88.1 us
    pallas_call x1, Pallas kernels: 89 us -> 87.1 us  [per_device(): pl.pallas_call(functools.partial(kernel, sizes), out_shape=(pltpu.VMEM((s...]
where the time goes in v2:
time: 88.9 us; the launch traced here: 88.8 us
  Pallas kernels  88.1 us (99%)
    pallas_call x1, Pallas kernels, per_device(): pl.pallas_call(functools.partial(kernel, sizes), out_shape=(pltpu.VMEM((s...  87.1 us

profile of v2, /device:TPU:230, one launch (start us, length us, event | category | flops | bytes accessed | tf_op | source)
XLA Modules:
  0.0 88.8 jit_solution(12376754742213112042)
XLA Ops:
  0.6 87.1 %chain.1 = (bf16[32,1024]{1,0:T(8,128)(2,1)S(1)}, bf16[32,64,256]{2,1,0:T(8,128)(2,1)S(1)}) custom-call(s32[32]{0:T(128)} %lens_in.1, s32[3,6]{1,0:T(4,128)} %bitcast.1, bf16[32,4096]{1,0:T(8,128)(2,1)} %hidden.1, bf16[1,32,1024]{2,1,0:T(8,128)(2,1)} %query.1, bf16[1,32,64,256]{3,2,1,0:T(8,128)(2,1)} %cache.1, f32[1,4096]{1,0:T(1,128)} %gain.1, ...), custom_call_target="tpu_custom_call" | custom-call | tf_op jit(solution)/shard_map/chain/pallas_call | solution.py:598
  87.7 1.0 %finish.1 = (bf16[1,32,1024]{2,1,0:T(8,128)(2,1)}, bf16[1,32,64,256]{3,2,1,0:T(8,128)(2,1)}) custom-call(bf16[32,1024]{1,0:T(8,128)(2,1)S(1)} %get-tuple-element.4.xout, bf16[32,64,256]{2,1,0:T(8,128)(2,1)S(1)} %get-tuple-element.5.base), custom_call_target="tpu_custom_call" | custom-call | tf_op jit(solution)/shard_map/finish/pallas_call | solution.py:652

commit v3 on v2

--- a/solution.py
+++ b/solution.py
@@ -352,15 +352,11 @@
                 jnp.concatenate(scaled, axis=1), kvw_v[h], preferred_element_type=F32)
         fresh = (acc * lax.rsqrt(square * (1.0 / width) + 1e-06)).astype(BF16).astype(F32)
         fresh_f[rows, :] = fresh
-
-    def front(m):
+        return fresh
+
+    def front(m, head):
         rows = pl.ds(pl.multiple_of(m * R, R), R)
-
-        @pl.when(l > 0)
-        def _():
-            fresh_part(m)
-
-        fresh = fresh_f[rows, :]
+        fresh = fresh_f[rows, :] if head else fresh_part(m)
         key = fresh[:, 0:HD]
         value = fresh[:, HD:2 * HD]
         parts = []
@@ -463,55 +459,63 @@
     def _():
         arrive()
 
+    def weights_wait():
+        for h in range(H):
+            for d in order + (0,):
+                outw_load(h, d).wait()
+
+    def batch(m, head):
+        context = front(m, head)
+
+        if head:
+
+            @pl.when(m == 0)
+            def _():
+                weights_wait()
+                pl.semaphore_wait(barrier, T - 1 + G - 1 + T)
+
+        for h in range(H):
+            project(m, context, h)
+        for h in range(H):
+            project_own(m, context, h)
+
+        if head:
+
+            @pl.when(m == 0)
+            def _():
+                attend(first, blocks)
+
+        else:
+
+            @pl.when(m + 1 < micros)
+            def _():
+                forward(m + 1)
+
+            @pl.when((l == last) & (m == micros - 1))
+            def _():
+                collect()
+                settle()
+
+        for h in range(H):
+            reduce(m, h)
+
+        if not head:
+
+            @pl.when((l == last) & (m == 0))
+            def _():
+                exchange()
+
+    @pl.when(l == 0)
+    def _():
+        lax.fori_loop(0, micros, lambda m, carry: batch(m, True) or carry, 0)
+
     @pl.when(l > 0)
     def _():
         gain_load.wait()
         arrived(kvw_v, load_sem.at[3])
-
-    forward(0)
-
-    def batch(m, carry):
-        context = front(m)
-
-        @pl.when((l == 0) & (m == 0))
-        def _():
-            pl.semaphore_wait(barrier, T - 1 + G - 1 + T)
-
-        @pl.when(m == 0)
-        def _():
-            for h in range(H):
-                for d in order + (0,):
-                    outw_load(h, d).wait()
-
-        for h in range(H):
-            project(m, context, h)
-
-        @pl.when(m + 1 < micros)
-        def _():
-            forward(m + 1)
-
-        for h in range(H):
-            project_own(m, context, h)
-
-        @pl.when((l == 0) & (m == 0))
-        def _():
-            attend(first, blocks)
-
-        @pl.when((l == last) & (m == micros - 1))
-        def _():
-            collect()
-            settle()
-
-        for h in range(H):
-            reduce(m, h)
-
-        @pl.when((l == last) & (m == 0))
-        def _():
-            exchange()
-
-        return carry
-
-    lax.fori_loop(0, micros, batch, 0)
+        weights_wait()
+        forward(0)
+        lax.fori_loop(0, micros, lambda m, carry: batch(m, False) or carry, 0)
 
     @pl.when(l == 0)
     def _():

time: 88.9 us -> 91.3 us (1.027)
  Pallas kernels: 88.1 us -> 90.3 us
    pallas_call x1, Pallas kernels: 87.1 us -> 89.3 us  [per_device(): pl.pallas_call(functools.partial(kernel, sizes), out_shape=(pltpu.VMEM((s...]
where the time goes in v3:
time: 91.3 us; the launch traced here: 91 us
  Pallas kernels  90.3 us (99%)
    pallas_call x1, Pallas kernels, per_device(): pl.pallas_call(functools.partial(kernel, sizes), out_shape=(pltpu.VMEM((s...  89.3 us

profile of v3, /device:TPU:230, one launch (start us, length us, event | category | flops | bytes accessed | tf_op | source)
XLA Modules:
  0.0 91.0 jit_solution(13978091384793928252)
XLA Ops:
  0.6 89.3 %chain.1 = (bf16[32,1024]{1,0:T(8,128)(2,1)S(1)}, bf16[32,64,256]{2,1,0:T(8,128)(2,1)S(1)}) custom-call(s32[32]{0:T(128)} %lens_in.1, s32[3,6]{1,0:T(4,128)} %bitcast.1, bf16[32,4096]{1,0:T(8,128)(2,1)} %hidden.1, bf16[1,32,1024]{2,1,0:T(8,128)(2,1)} %query.1, bf16[1,32,64,256]{3,2,1,0:T(8,128)(2,1)} %cache.1, f32[1,4096]{1,0:T(1,128)} %gain.1, ...), custom_call_target="tpu_custom_call" | custom-call | tf_op jit(solution)/shard_map/chain/pallas_call | solution.py:602
  90.0 1.0 %finish.1 = (bf16[1,32,1024]{2,1,0:T(8,128)(2,1)}, bf16[1,32,64,256]{3,2,1,0:T(8,128)(2,1)}) custom-call(bf16[32,1024]{1,0:T(8,128)(2,1)S(1)} %get-tuple-element.4.xout, bf16[32,64,256]{2,1,0:T(8,128)(2,1)S(1)} %get-tuple-element.5.base), custom_call_target="tpu_custom_call" | custom-call | tf_op jit(solution)/shard_map/finish/pallas_call | solution.py:656

commit v4 on v2

--- a/solution.py
+++ b/solution.py
@@ -121,12 +121,6 @@
             pltpu.make_async_copy(
                 kvw.at[0, pl.ds(q * W + h * S, S)], kvw_v.at[h, pl.ds(q * S, S)],
                 load_sem.at[3]).start()
-
-    for h in range(H):
-        for d in order:
-            outw_load(h, d).start()
-    for h in range(H):
-        outw_load(h, 0).start()
 
     barrier = pltpu.get_barrier_semaphore()
     for d in range(1, T):
@@ -441,11 +435,16 @@
     lens_load.wait()
     moves_load.wait()
     arrange()
+    for h in range(H):
+        for d in order:
+            outw_load(h, d).start()
     query_load.wait()
     cache_load.wait()
     qf_v[...] = jnp.dot(pick_ref[...], q_v[...], preferred_element_type=F32)
     first = R // block
     attend(0, first)
+    for h in range(H):
+        outw_load(h, 0).start()
 
     @pl.when(l > 0)
     def _():

time: 88.9 us -> 88.8 us (level)
  no operation moved by 1% of the time
where the time goes in v4:
time: 88.8 us; the launch traced here: 88.7 us
  Pallas kernels  88.1 us (99%)
    pallas_call x1, Pallas kernels, per_device(): pl.pallas_call(functools.partial(kernel, sizes), out_shape=(pltpu.VMEM((s...  87.1 us

profile of v4, /device:TPU:230, one launch (start us, length us, event | category | flops | bytes accessed | tf_op | source)
XLA Modules:
  0.0 88.7 jit_solution(6234442626581343791)
XLA Ops:
  0.6 87.1 %chain.1 = (bf16[32,1024]{1,0:T(8,128)(2,1)S(1)}, bf16[32,64,256]{2,1,0:T(8,128)(2,1)S(1)}) custom-call(s32[32]{0:T(128)} %lens_in.1, s32[3,6]{1,0:T(4,128)} %bitcast.1, bf16[32,4096]{1,0:T(8,128)(2,1)} %hidden.1, bf16[1,32,1024]{2,1,0:T(8,128)(2,1)} %query.1, bf16[1,32,64,256]{3,2,1,0:T(8,128)(2,1)} %cache.1, f32[1,4096]{1,0:T(1,128)} %gain.1, ...), custom_call_target="tpu_custom_call" | custom-call | tf_op jit(solution)/shard_map/chain/pallas_call | solution.py:597
  87.7 1.0 %finish.1 = (bf16[1,32,1024]{2,1,0:T(8,128)(2,1)}, bf16[1,32,64,256]{3,2,1,0:T(8,128)(2,1)}) custom-call(bf16[32,1024]{1,0:T(8,128)(2,1)S(1)} %get-tuple-element.4.xout, bf16[32,64,256]{2,1,0:T(8,128)(2,1)S(1)} %get-tuple-element.5.base), custom_call_target="tpu_custom_call" | custom-call | tf_op jit(solution)/shard_map/finish/pallas_call | solution.py:651

commit v5 on v4

--- a/solution.py
+++ b/solution.py
@@ -432,6 +432,28 @@
                 base_v[j, :, cols] = jnp.where(
                     here, fresh[j:j + 1, :], base_v[j, :, cols].astype(F32)).astype(BF16)
 
+    def emit(h):
+        cols = slice(h * S, (h + 1) * S)
+        kept = jnp.dot(
+            back_ref[...], xnew_f[:, cols].astype(BF16), preferred_element_type=F32)
+        for k in range(S // HD):
+            c = h * (S // HD) + k
+            xout_ref[:, c * HD:(c + 1) * HD] = (
+                kept[:, k * HD:(k + 1) * HD] + moved_ref[c * slots:(c + 1) * slots, :]).astype(BF16)
+
+    def rs_sent(m):
+        for h in range(H):
+            for d in order:
+                rs_copy(m, h, d).wait_send()
+
+    def sent():
+        for m in range(micros - 1):
+            rs_sent(m)
+        for d in range(1, G):
+            info_copy(d).wait_send()
+            gc_copy(d).wait_send()
+            row_copy(d).wait_send()
+
     lens_load.wait()
     moves_load.wait()
     arrange()
@@ -500,9 +522,15 @@
         def _():
             collect()
             settle()
+            sent()
 
         for h in range(H):
             reduce(m, h)
+            if h < H - 1:
+
+                @pl.when((l == last) & (m == micros - 1))
+                def _():
+                    emit(h)
 
         @pl.when((l == last) & (m == 0))
         def _():
@@ -526,19 +554,18 @@
         collect()
         settle()
 
-    kept = jnp.dot(back_ref[...], xnew_f[...].astype(BF16), preferred_element_type=F32)
-    for c in range(heads):
-        cols = slice(c * HD, (c + 1) * HD)
-        xout_ref[:, cols] = (kept[:, cols] + moved_ref[c * slots:(c + 1) * slots, :]).astype(BF16)
-
-    for m in range(micros):
-        for h in range(H):
-            for d in order:
-                rs_copy(m, h, d).wait_send()
-    for d in range(1, G):
-        info_copy(d).wait_send()
-        gc_copy(d).wait_send()
-        row_copy(d).wait_send()
+    @pl.when(l < last)
+    def _():
+        for h in range(H - 1):
+            emit(h)
+
+    emit(H - 1)
+
+    @pl.when(l < last)
+    def _():
+        sent()
+
+    rs_sent(micros - 1)
 
     @pl.when((l < last) & (l != half - 1))
     def _():

time: 88.8 us -> 88.7 us (level)
  no operation moved by 1% of the time
where the time goes in v5:
time: 88.7 us; the launch traced here: 88.6 us
  Pallas kernels  88 us (99%)
    pallas_call x1, Pallas kernels, per_device(): pl.pallas_call(functools.partial(kernel, sizes), out_shape=(pltpu.VMEM((s...  87 us

profile of v5, /device:TPU:230, one launch (start us, length us, event | category | flops | bytes accessed | tf_op | source)
XLA Modules:
  0.0 88.6 jit_solution(14220793721035124865)
XLA Ops:
  0.6 87.0 %chain.1 = (bf16[32,1024]{1,0:T(8,128)(2,1)S(1)}, bf16[32,64,256]{2,1,0:T(8,128)(2,1)S(1)}) custom-call(s32[32]{0:T(128)} %lens_in.1, s32[3,6]{1,0:T(4,128)} %bitcast.1, bf16[32,4096]{1,0:T(8,128)(2,1)} %hidden.1, bf16[1,32,1024]{2,1,0:T(8,128)(2,1)} %query.1, bf16[1,32,64,256]{3,2,1,0:T(8,128)(2,1)} %cache.1, f32[1,4096]{1,0:T(1,128)} %gain.1, ...), custom_call_target="tpu_custom_call" | custom-call | tf_op jit(solution)/shard_map/chain/pallas_call | solution.py:624
  87.6 1.0 %finish.1 = (bf16[1,32,1024]{2,1,0:T(8,128)(2,1)}, bf16[1,32,64,256]{3,2,1,0:T(8,128)(2,1)}) custom-call(bf16[32,1024]{1,0:T(8,128)(2,1)S(1)} %get-tuple-element.4.xout, bf16[32,64,256]{2,1,0:T(8,128)(2,1)S(1)} %get-tuple-element.5.base), custom_call_target="tpu_custom_call" | custom-call | tf_op jit(solution)/shard_map/finish/pallas_call | solution.py:678

commit v6 on v5

--- a/solution.py
+++ b/solution.py
@@ -374,11 +374,8 @@
         for i, d in enumerate(order):
             part = jnp.dot(
                 context, outw_v[h, :, i * S:(i + 1) * S], preferred_element_type=F32)
-            if i or h:
-                rs_copy(m, h if i else h - 1, order[i - 1]).start()
             rs_send[m, h, d - 1] = part.astype(BF16)
-        if h == H - 1:
-            rs_copy(m, h, order[-1]).start()
+            rs_copy(m, h, d).start()
 
     def project_own(m, context, h):
         own_part[m, h] = jnp.dot(

time: 88.7 us -> 90 us (1.015)
  Pallas kernels: 88 us -> 89 us
    pallas_call x1, Pallas kernels: 87 us -> 88 us  [per_device(): pl.pallas_call(functools.partial(kernel, sizes), out_shape=(pltpu.VMEM((s...]
where the time goes in v6:
time: 90 us; the launch traced here: 89.7 us
  Pallas kernels  89 us (99%)
    pallas_call x1, Pallas kernels, per_device(): pl.pallas_call(functools.partial(kernel, sizes), out_shape=(pltpu.VMEM((s...  88 us

profile of v6, /device:TPU:230, one launch (start us, length us, event | category | flops | bytes accessed | tf_op | source)
XLA Modules:
  0.0 89.7 jit_solution(755969621942888607)
XLA Ops:
  0.6 88.0 %chain.1 = (bf16[32,1024]{1,0:T(8,128)(2,1)S(1)}, bf16[32,64,256]{2,1,0:T(8,128)(2,1)S(1)}) custom-call(s32[32]{0:T(128)} %lens_in.1, s32[3,6]{1,0:T(4,128)} %bitcast.1, bf16[32,4096]{1,0:T(8,128)(2,1)} %hidden.1, bf16[1,32,1024]{2,1,0:T(8,128)(2,1)} %query.1, bf16[1,32,64,256]{3,2,1,0:T(8,128)(2,1)} %cache.1, f32[1,4096]{1,0:T(1,128)} %gain.1, ...), custom_call_target="tpu_custom_call" | custom-call | tf_op jit(solution)/shard_map/chain/pallas_call | solution.py:621
  88.6 1.0 %finish.1 = (bf16[1,32,1024]{2,1,0:T(8,128)(2,1)}, bf16[1,32,64,256]{3,2,1,0:T(8,128)(2,1)}) custom-call(bf16[32,1024]{1,0:T(8,128)(2,1)S(1)} %get-tuple-element.4.xout, bf16[32,64,256]{2,1,0:T(8,128)(2,1)S(1)} %get-tuple-element.5.base), custom_call_target="tpu_custom_call" | custom-call | tf_op jit(solution)/shard_map/finish/pallas_call | solution.py:675

commit v7 on v5

--- a/solution.py
+++ b/solution.py
@@ -106,21 +106,21 @@
     movers = moves_ref.shape[1]
     place_load = pltpu.make_async_copy(place_v.at[0], place_s, local_sem.at[0])
 
-    lens_load.start()
-    moves_load.start()
-    query_load.start()
-    cache_load.start()
+    lens_load.start(priority=1)
+    moves_load.start(priority=1)
+    query_load.start(priority=1)
+    cache_load.start(priority=1)
 
     @pl.when(l == 0)
     def _():
-        x_load.start()
-
-    gain_load.start()
+        x_load.start(priority=1)
+
+    gain_load.start(priority=1)
     for h in range(H):
         for q in range(T):
             pltpu.make_async_copy(
                 kvw.at[0, pl.ds(q * W + h * S, S)], kvw_v.at[h, pl.ds(q * S, S)],
-                load_sem.at[3]).start()
+                load_sem.at[3]).start(priority=1)
 
     barrier = pltpu.get_barrier_semaphore()
     for d in range(1, T):

time: 88.7 us -> 88.6 us (level)
  no operation moved by 1% of the time
where the time goes in v7:
time: 88.6 us; the launch traced here: 88.5 us
  Pallas kernels  87.9 us (99%)
    pallas_call x1, Pallas kernels, per_device(): pl.pallas_call(functools.partial(kernel, sizes), out_shape=(pltpu.VMEM((s...  86.9 us

profile of v7, /device:TPU:230, one launch (start us, length us, event | category | flops | bytes accessed | tf_op | source)
XLA Modules:
  0.0 88.5 jit_solution(15605891503518946045)
XLA Ops:
  0.6 86.9 %chain.1 = (bf16[32,1024]{1,0:T(8,128)(2,1)S(1)}, bf16[32,64,256]{2,1,0:T(8,128)(2,1)S(1)}) custom-call(s32[32]{0:T(128)} %lens_in.1, s32[3,6]{1,0:T(4,128)} %bitcast.1, bf16[32,4096]{1,0:T(8,128)(2,1)} %hidden.1, bf16[1,32,1024]{2,1,0:T(8,128)(2,1)} %query.1, bf16[1,32,64,256]{3,2,1,0:T(8,128)(2,1)} %cache.1, f32[1,4096]{1,0:T(1,128)} %gain.1, ...), custom_call_target="tpu_custom_call" | custom-call | tf_op jit(solution)/shard_map/chain/pallas_call | solution.py:624
  87.5 1.0 %finish.1 = (bf16[1,32,1024]{2,1,0:T(8,128)(2,1)}, bf16[1,32,64,256]{3,2,1,0:T(8,128)(2,1)}) custom-call(bf16[32,1024]{1,0:T(8,128)(2,1)S(1)} %get-tuple-element.4.xout, bf16[32,64,256]{2,1,0:T(8,128)(2,1)S(1)} %get-tuple-element.5.base), custom_call_target="tpu_custom_call" | custom-call | tf_op jit(solution)/shard_map/finish/pallas_call | solution.py:678

commit v8 on v7

--- a/solution.py
+++ b/solution.py
@@ -121,6 +121,10 @@
             pltpu.make_async_copy(
                 kvw.at[0, pl.ds(q * W + h * S, S)], kvw_v.at[h, pl.ds(q * S, S)],
                 load_sem.at[3]).start(priority=1)
+
+    for h in range(H):
+        for d in order:
+            outw_load(h, d).start()
 
     barrier = pltpu.get_barrier_semaphore()
     for d in range(1, T):
@@ -457,9 +461,6 @@
     lens_load.wait()
     moves_load.wait()
     arrange()
-    for h in range(H):
-        for d in order:
-            outw_load(h, d).start()
     query_load.wait()
     cache_load.wait()
     qf_v[...] = jnp.dot(pick_ref[...], q_v[...], preferred_element_type=F32)

time: 88.6 us -> 89.3 us (level)
  no operation moved by 1% of the time
where the time goes in v8:
time: 89.3 us; the launch traced here: 89 us
  Pallas kernels  88.4 us (99%)
    pallas_call x1, Pallas kernels, per_device(): pl.pallas_call(functools.partial(kernel, sizes), out_shape=(pltpu.VMEM((s...  87.3 us

profile of v8, /device:TPU:230, one launch (start us, length us, event | category | flops | bytes accessed | tf_op | source)
XLA Modules:
  0.0 89.0 jit_solution(107381582092685824)
XLA Ops:
  0.6 87.3 %chain.1 = (bf16[32,1024]{1,0:T(8,128)(2,1)S(1)}, bf16[32,64,256]{2,1,0:T(8,128)(2,1)S(1)}) custom-call(s32[32]{0:T(128)} %lens_in.1, s32[3,6]{1,0:T(4,128)} %bitcast.1, bf16[32,4096]{1,0:T(8,128)(2,1)} %hidden.1, bf16[1,32,1024]{2,1,0:T(8,128)(2,1)} %query.1, bf16[1,32,64,256]{3,2,1,0:T(8,128)(2,1)} %cache.1, f32[1,4096]{1,0:T(1,128)} %gain.1, ...), custom_call_target="tpu_custom_call" | custom-call | tf_op jit(solution)/shard_map/chain/pallas_call | solution.py:625
  88.0 1.0 %finish.1 = (bf16[1,32,1024]{2,1,0:T(8,128)(2,1)}, bf16[1,32,64,256]{3,2,1,0:T(8,128)(2,1)}) custom-call(bf16[32,1024]{1,0:T(8,128)(2,1)S(1)} %get-tuple-element.4.xout, bf16[32,64,256]{2,1,0:T(8,128)(2,1)S(1)} %get-tuple-element.5.base), custom_call_target="tpu_custom_call" | custom-call | tf_op jit(solution)/shard_map/finish/pallas_call | solution.py:679

commit v9 on v7

--- a/solution.py
+++ b/solution.py
@@ -49,17 +49,20 @@
 
     order = tuple(sorted(range(1, T), key=lambda d: -min(d, T - d)))
 
+    def turned(d):
+        return lax.rem(t + T + (1 - 2 * lax.rem(g, 2)) * d, T)
+
     def rs_copy(m, h, d):
         return pltpu.make_async_remote_copy(
             src_ref=rs_send.at[m, h, d - 1], dst_ref=rs_recv.at[m, h, d - 1],
             send_sem=rs_ss.at[m, h, d - 1], recv_sem=rs_rs.at[m, h],
-            device_id={"tensor": lax.rem(t + d, T)}, device_id_type=MESH)
+            device_id={"tensor": turned(d)}, device_id_type=MESH)
 
     def ag_copy(m, h, d):
         return pltpu.make_async_remote_copy(
             src_ref=xnew.at[m, h], dst_ref=xin.at[m, h, t],
             send_sem=ag_ss.at[m, h, d], recv_sem=ag_rs.at[m, h],
-            device_id={"section": l + 1, "tensor": lax.rem(t + d, T)}, device_id_type=MESH)
+            device_id={"section": l + 1, "tensor": turned(d)}, device_id_type=MESH)
 
     def hop_copy(m, h):
         return pltpu.make_async_remote_copy(
@@ -71,7 +74,7 @@
         return pltpu.make_async_remote_copy(
             src_ref=xin.at[m, h, t], dst_ref=xin.at[m, h, t],
             send_sem=fwd_ss.at[m, h, d - 1], recv_sem=ag_rs.at[m, h],
-            device_id={"tensor": lax.rem(t + d, T)}, device_id_type=MESH)
+            device_id={"tensor": turned(d)}, device_id_type=MESH)
 
     def arrived(ref, sem):
         pltpu.make_async_copy(ref, ref, sem).wait()
@@ -92,7 +95,7 @@
         return to_group(row_pack.at[d - 1], row_arr.at[d - 1], row_ss, row_rs, d)
 
     def outw_load(h, d):
-        start = pl.multiple_of(lax.rem(t + d, T) * W + h * S, S)
+        start = pl.multiple_of(turned(d) * W + h * S, S)
         place = order.index(d) if d else T - 1
         return pltpu.make_async_copy(
             outw.at[0, :, pl.ds(start, S)], outw_v.at[h, :, pl.ds(place * S, S)], outw_sem.at[h, d])

time: 88.6 us -> 88.8 us (level)
  no operation moved by 1% of the time
where the time goes in v9:
time: 88.8 us; the launch traced here: 88.7 us
  Pallas kernels  88.1 us (99%)
    pallas_call x1, Pallas kernels, per_device(): pl.pallas_call(functools.partial(kernel, sizes), out_shape=(pltpu.VMEM((s...  87.1 us

profile of v9, /device:TPU:230, one launch (start us, length us, event | category | flops | bytes accessed | tf_op | source)
XLA Modules:
  0.0 88.7 jit_solution(11968908993668764283)
XLA Ops:
  0.6 87.1 %chain.1 = (bf16[32,1024]{1,0:T(8,128)(2,1)S(1)}, bf16[32,64,256]{2,1,0:T(8,128)(2,1)S(1)}) custom-call(s32[32]{0:T(128)} %lens_in.1, s32[3,6]{1,0:T(4,128)} %bitcast.1, bf16[32,4096]{1,0:T(8,128)(2,1)} %hidden.1, bf16[1,32,1024]{2,1,0:T(8,128)(2,1)} %query.1, bf16[1,32,64,256]{3,2,1,0:T(8,128)(2,1)} %cache.1, f32[1,4096]{1,0:T(1,128)} %gain.1, ...), custom_call_target="tpu_custom_call" | custom-call | tf_op jit(solution)/shard_map/chain/pallas_call | solution.py:627
  87.7 1.0 %finish.1 = (bf16[1,32,1024]{2,1,0:T(8,128)(2,1)}, bf16[1,32,64,256]{3,2,1,0:T(8,128)(2,1)}) custom-call(bf16[32,1024]{1,0:T(8,128)(2,1)S(1)} %get-tuple-element.4.xout, bf16[32,64,256]{2,1,0:T(8,128)(2,1)S(1)} %get-tuple-element.5.base), custom_call_target="tpu_custom_call" | custom-call | tf_op jit(solution)/shard_map/finish/pallas_call | solution.py:681
